TPU v7x, 32 devices: a whole 2x2x4 slice. The times are simulated.
32 devices in a mesh: chan: 8 (over z, y), orb: 4 (over x, core).
Axes of the slice: x: 2, y: 2, z: 4, core: 2. Of those that a mesh axis runs over, the one named last changes fastest.
Arguments:
- amplitudes: bfloat16 [20480, 1024], P(('chan', 'orb')), may hold values from -6 to 6
- recoupling: float32 [20480], P(('chan', 'orb')), may hold values from -1.5 to 1.5
- denominators: float32 [20480], P(('chan', 'orb')), may hold values from 1 to 8
- interaction: bfloat16 [32, 1024, 1024], P('chan', 'orb'), may hold values from -0.25 to 0.25
- pair_source: int32 [32, 1024], P('chan', 'orb'), may hold values from -1 to 639, as said below
- return_slot: int32 [20480], P(('chan', 'orb')), may hold values from 0 to 1023, as said below
- channel_sizes: int32 [32], P('chan'), may hold values from 256 to 1024, as said below
Outputs:
- updated: bfloat16 [20480, 1024], P(('chan', 'orb'))
Inputs may be any that keep to these rules, and one draw needn't show every extreme that they name: `channel_sizes`: every channel size is a multiple of 4; the 4 sizes of blocks c with the same c div 4 sum to 2560. pair_source[c, p] = -1 exactly where live[c, p] = 0. For each e and o, over the blocks c with c div 4 = e and the positions p with p div 256 = o, the other values name each number 0 to 639 once. return_slot[(e * 4 + o) * 640 + i] is the k with pair_source[e * 4 + k div 256, o * 256 + k mod 256] = i.
All inputs are finite; a program needn't handle non-finite values.
Results may differ from a plain program's by a relative error of at most 0.002.
Values may be sent and summed in bfloat16 or wider, within the bound.
A program may use at most 64 MiB of HBM per device.

v0:
```python
import jax
import jax.numpy as jnp
from jax import lax
from jax.sharding import PartitionSpec as P


def shards(
    amplitudes, recoupling, denominators, interaction, pair_source, return_slot, channel_sizes
):
    chan_count = lax.axis_size("chan")
    orb_count = lax.axis_size("orb")
    row_count = amplitudes.shape[0]
    width = amplitudes.shape[1]
    per_peer = row_count // chan_count
    blocks_here = pair_source.shape[0]
    rows_block = pair_source.shape[1]
    relayed = (amplitudes.astype(jnp.float32) * recoupling[:, None]).astype(jnp.bfloat16)
    received = lax.all_to_all(
        relayed.reshape(chan_count, per_peer, width),
        "chan",
        split_axis=0,
        concat_axis=0,
        tiled=True,
    )
    received = received.reshape(row_count, width)
    flat_source = pair_source.reshape(-1)
    amp_rows = jnp.take(received, jnp.maximum(flat_source, 0), axis=0)
    position = jnp.arange(width, dtype=jnp.int32)
    pair_rank = orb_count * (position % rows_block) + position // rows_block
    live_mask = pair_rank[None, :] < channel_sizes[:, None]
    keep = (pair_source >= 0)[:, :, None] & live_mask[:, None, :]
    amp_block = jnp.where(
        keep, amp_rows.reshape(blocks_here, rows_block, width), jnp.zeros((), jnp.bfloat16)
    )
    cycle_local = jnp.einsum(
        "bik,bkj->bij",
        interaction,
        lax.all_gather(amp_block, "orb", axis=1, tiled=True),
        preferred_element_type=jnp.float32,
    ).astype(jnp.bfloat16)
    outgoing = jnp.take(cycle_local.reshape(blocks_here * rows_block, width), return_slot, axis=0)
    returned = lax.all_to_all(
        outgoing.reshape(chan_count, per_peer, width),
        "chan",
        split_axis=0,
        concat_axis=0,
        tiled=True,
    )
    returned = returned.reshape(row_count, width)
    updated = (
        amplitudes.astype(jnp.float32)
        + recoupling[:, None] * returned.astype(jnp.float32) / denominators[:, None]
    )
    return updated.astype(jnp.bfloat16)


def solution(mesh):
    in_specs = (
        P(("chan", "orb"), None),
        P(("chan", "orb")),
        P(("chan", "orb")),
        P("chan", "orb", None),
        P("chan", "orb"),
        P(("chan", "orb")),
        P("chan"),
    )
    out_specs = P(("chan", "orb"), None)
    return jax.shard_map(shards, mesh=mesh, in_specs=in_specs, out_specs=out_specs, check_vma=False)
```

profile of v0, /device:TPU:0, one launch (start us, length us, event | category | flops | bytes accessed | tf_op | source)
XLA Modules:
  0.0 172.8 jit_solution(11836491598782598001)
XLA Ops:
  6.5 0.0 copy-start
  6.5 2.8 %fusion = bf16[640,1024]{1,0:T(8,128)(2,1)} fusion(bf16[640,1024]{1,0:T(8,128)(2,1)} %param.7, f32[640]{0:T(1024)} %param.8), kind=kLoop, calls=%fused_computation.5 | loop fusion | flops 1966080 | bytes 2624000 | tf_op jit(solution)/shard_map/convert_element_type | solution.py:17
  9.3 7.3 %all-to-all-start = ((bf16[8,80,1024]{2,1,0:T(8,128)(2,1)}), bf16[8,80,1024]{2,1,0:T(8,128)(2,1)S(1)}, u32[]{:S(2)}, u32[]{:S(2)}) async-start(bf16[8,80,1024]{2,1,0:T(8,128)(2,1)} %bitcast.18), calls=%async_computation | async-start | bytes 2621440 | tf_op jit(solution)/shard_map/all_to_all | solution.py:18
  16.6 0.0 all-gather.2.cloned.1.call-start
  16.7 0.0 copy-done.3
  16.7 0.0 copy-done.6
  16.8 0.1 broadcast_compare_fusion
  16.8 31.2 %all-to-all-done = bf16[8,80,1024]{2,1,0:T(8,128)(2,1)S(1)} async-done(((bf16[8,80,1024]{2,1,0:T(8,128)(2,1)}), bf16[8,80,1024]{2,1,0:T(8,128)(2,1)S(1)}, u32[]{:S(2)}, u32[]{:S(2)}) %all-to-all-start) | async-done | bytes 1310752 | tf_op jit(solution)/shard_map/all_to_all | solution.py:18
  48.0 5.4 %gather_fusion = bf16[1024,1024]{1,0:T(8,128)(2,1)} fusion(bf16[640,1024]{1,0:T(8,128)(2,1)S(1)} %bitcast.15, s32[1024]{0:T(1024)S(1)} %broadcast_clamp_fusion), kind=kCustom, calls=%fused_computation | custom fusion | bytes 4198400 | tf_op jit(solution)/shard_map/jit(_take)/gather | solution.py:27
  53.4 3.1 %and_select_fusion = bf16[4,256,1024]{2,1,0:T(8,128)(2,1)} fusion(bf16[4,256,1024]{2,1,0:T(8,128)(2,1)} %bitcast.17, pred[4,256]{1,0:T(4,128)(4,1)S(1)} %get-tuple-element.6, pred[4,1024]{1,0:T(4,128)(4,1)S(1)} %broadcast_compare_fusion, pred[4,256]{1,0:T(4,128)(4,1)S(1)} %get-tuple-element.5), kind=kLoop, calls=%fused_computation.2 | loop fusion | flops 3145728 | bytes 4200448 | tf_op jit(solution)/shard_map/jit(_where)/select_n | solution.py:32
  56.5 0.0 all-gather.2.cloned.1.call-update
  56.5 0.7 copy-done.2
  57.2 0.1 broadcast_in_dim.35
  57.3 56.7 %all-gather.2.cloned.1.call-done = bf16[4,1024,1024]{2,1,0:T(8,128)(2,1)} async-done(((bf16[4,256,1024]{2,1,0:T(8,128)(2,1)}), bf16[4,1024,1024]{2,1,0:T(8,128)(2,1)}) %all-gather.2.cloned.1.call-update) | async-done | bytes 8388624 | tf_op jit(solution)/shard_map/all_gather | solution.py:38
  114.0 0.0 copy-done
  114.0 7.1 %convolution_convert_fusion = bf16[4,1024,256]{1,2,0:T(8,128)(2,1)} fusion(bf16[4,256,1024]{2,1,0:T(8,128)(2,1)S(1)} %copy-done, bf16[4,1024,1024]{2,1,0:T(8,128)(2,1)} %all-gather.2.cloned.1.call-done), kind=kOutput, calls=%fused_computation.9 | convolution fusion | flops 2148532224 | bytes 12582912 | tf_op jit(solution)/shard_map/bik,bkj->bij/dot_general | solution.py:35
  121.1 5.7 %gather_fusion.1 = bf16[640,1024]{1,0:T(8,128)(2,1)S(1)} fusion(bf16[1024,1024]{1,0:T(8,128)(2,1)} %bitcast.16, s32[1024]{0:T(1024)S(1)} %pad_clamp_fusion), kind=kCustom, calls=%fused_computation.1 | custom fusion | bytes 2624000 | tf_op jit(solution)/shard_map/jit(_take)/gather | solution.py:41
  126.9 0.0 copy-start.1
  126.9 0.0 copy-start.4
  126.9 0.0 copy-start.5
  126.9 0.2 broadcast_select_fusion
  127.1 37.2 %all_to_all.10 = bf16[8,80,1024]{2,1,0:T(8,128)(2,1)S(1)} all-to-all(bf16[8,80,1024]{2,1,0:T(8,128)(2,1)S(1)} %broadcast_select_fusion), channel_id=1, replica_groups=mesh['chan'=8,'orb'=4] {'chan'}, dimensions={0} | all-to-all | bytes 2621440 | tf_op jit(solution)/shard_map/all_to_all | solution.py:42
  164.3 0.0 copy-done.1
  164.3 1.6 fusion.1
  (13 shorter events, 0.1 us)
Async XLA Ops:
  6.5 107.5 %copy-start = (bf16[4,256,1024]{2,1,0:T(8,128)(2,1)S(1)}, bf16[4,256,1024]{2,1,0:T(8,128)(2,1)}, u32[]{:S(2)}) copy-start(bf16[4,256,1024]{2,1,0:T(8,128)(2,1)} %param.10) | copy-start | bytes 6291460
  6.5 10.1 %copy-start.3 = (s32[4,256]{1,0:T(4,128)S(1)}, s32[4,256]{1,0:T(4,128)}, u32[]{:S(2)}) copy-start(s32[4,256]{1,0:T(4,128)} %param.11) | copy-start | bytes 12292
  6.5 10.2 %copy-start.6 = (s32[4]{0:T(128)S(1)}, s32[4]{0:T(128)}, u32[]{:S(2)}) copy-start(s32[4]{0:T(128)} %param.13) | copy-start | bytes 52
  9.3 38.7 %all-to-all-start = ((bf16[8,80,1024]{2,1,0:T(8,128)(2,1)}), bf16[8,80,1024]{2,1,0:T(8,128)(2,1)S(1)}, u32[]{:S(2)}, u32[]{:S(2)}) async-start(bf16[8,80,1024]{2,1,0:T(8,128)(2,1)} %bitcast.18), calls=%async_computation | async-start | bytes 2621440 | tf_op jit(solution)/shard_map/all_to_all | solution.py:18
  16.6 97.4 %all-gather.2.cloned.1.call-start = ((), (), s32[]{:S(2)}) async-start(), calls=%async_computation.2 | async-start | bytes 10485760 | tf_op jit(solution)/shard_map/all_gather | solution.py:38
  56.5 0.7 copy-start.2
  126.9 37.4 %copy-start.1 = (bf16[640,1024]{1,0:T(8,128)(2,1)S(1)}, bf16[640,1024]{1,0:T(8,128)(2,1)}, u32[]{:S(2)}) copy-start(bf16[640,1024]{1,0:T(8,128)(2,1)} %param.7) | copy-start | bytes 3932164
  126.9 37.4 %copy-start.4 = (f32[640]{0:T(1024)S(1)}, f32[640]{0:T(1024)}, u32[]{:S(2)}) copy-start(f32[640]{0:T(1024)} %param.8) | copy-start | bytes 7684
  126.9 37.4 %copy-start.5 = (f32[640]{0:T(1024)S(1)}, f32[640]{0:T(1024)}, u32[]{:S(2)}) copy-start(f32[640]{0:T(1024)} %param.9) | copy-start | bytes 7684
Sparse Core Ops, SparseCore 0:
  56.7 57.3 all-gather.1
where the time goes:
time: 173 us
  waiting for transfers between devices  87.9 us (51%)
  blocking collectives  37.2 us (22%)
  between operations  13.5 us (8%)
  local copies, waits for them, and re-layouts  11.9 us (7%)
  other arithmetic  7.87 us (5%)
  starting transfers between devices  7.32 us (4%)
  matrix products  7.09 us (4%)
    all_gather x1, waiting for transfers between devices, shards(): lax.all_gather(amp_block, 'orb', axis=1, tiled=True)  56.7 us
    all_to_all x1, blocking collectives, shards(): lax.all_to_all(outgoing.reshape(chan_count, per_peer, width), 'chan', spl...  37.2 us
    all_to_all x1, waiting for transfers between devices, shards(): lax.all_to_all(relayed.reshape(chan_count, per_peer, width), 'chan', spli...  31.2 us
    all_to_all x1, starting transfers between devices, shards(): lax.all_to_all(relayed.reshape(chan_count, per_peer, width), 'chan', spli...  7.28 us
    dot_general x1, matrix products, shards(): jnp.einsum('bik,bkj->bij', interaction, lax.all_gather(amp_block, 'orb',...  7.09 us
    gather x1, local copies, waits for them, and re-layouts, shards(): jnp.take(cycle_local.reshape(blocks_here * rows_block, width), return_slo...  5.74 us
    gather x1, local copies, waits for them, and re-layouts, shards(): amp_rows = jnp.take(received, jnp.maximum(flat_source, 0), axis=0)  5.38 us
  transfers between devices with their start and end apart: 2, of which 2 were waited for; matrix products, arithmetic and copies ran while one was open for 0% of the time, Pallas kernels for 0%

commit v1 on v0

--- a/solution.py
+++ b/solution.py
@@ -1,12 +1,301 @@
+import functools
+
 import jax
 import jax.numpy as jnp
 from jax import lax
+from jax.experimental import pallas as pl
+from jax.experimental.pallas import tpu as pltpu
 from jax.sharding import PartitionSpec as P
 
-
-def shards(
-    amplitudes, recoupling, denominators, interaction, pair_source, return_slot, channel_sizes
+MESH = pl.DeviceIdType.MESH
+
+
+def peer_of(index, step, count):
+    total, bit = 0, 1
+    while bit < count:
+        digit = lax.rem(lax.div(index, bit), 2)
+        total = total + lax.rem(digit + (step // bit) % 2, 2) * bit
+        bit *= 2
+    return total
+
+
+def step_order(count):
+    steps = list(range(1, count))
+    far = [s for s in steps if s >= count // 2]
+    near = [s for s in steps if 1 < s < count // 2]
+    first = [s for s in steps if s == 1 and s < count // 2]
+    return first + far + near
+
+
+def kernel(
+    n_chan, n_orb, amp_ref, rec_ref, ps_ref, size_ref, w_ref, out_ref,
+    send_buf, recv_buf, ps_all, w_buf, mix, hot, picked, row_block, row_size, back_buf,
+    w_sem, ps_send, ps_recv, go_send, go_recv, cross_send, core_send, back_send, back_recv,
 ):
+    e = lax.axis_index("chan")
+    o = lax.axis_index("orb")
+    quota, width = send_buf.shape[1:]
+    rows = n_chan * quota
+    blocks, rows_block = w_buf.shape[:2]
+    local = blocks * rows_block
+    pairs = n_orb // 2
+    core = lax.rem(o, 2)
+    pair = lax.div(o, 2)
+    mate = o + 1 - 2 * core
+    tile = 2 * quota
+    order = step_order(n_chan)
+
+    w_copy = pltpu.make_async_copy(w_ref, w_buf, w_sem)
+    w_copy.start()
+
+    barrier = pltpu.get_barrier_semaphore()
+    for step in range(1, n_chan):
+        pl.semaphore_signal(
+            barrier, inc=1, device_id=(peer_of(e, step, n_chan), o), device_id_type=MESH
+        )
+    for step in range(1, n_orb):
+        pl.semaphore_signal(
+            barrier, inc=1, device_id=(e, lax.rem(o + step, n_orb)), device_id_type=MESH
+        )
+
+    def relay(d):
+        at = pl.ds(pl.multiple_of(d * quota, quota), quota)
+        return (amp_ref[at, :].astype(jnp.float32) * rec_ref[at, :]).astype(jnp.bfloat16)
+
+    recv_buf[o, e] = relay(e)
+
+    def fill(d, carry):
+        send_buf[d] = relay(d)
+        return carry
+
+    lax.fori_loop(0, n_chan, fill, 0)
+    ps_all[o] = ps_ref[...]
+    pl.semaphore_wait(barrier, n_chan + n_orb - 2)
+
+    def go(step):
+        d = peer_of(e, step, n_chan)
+        return pltpu.make_async_remote_copy(
+            src_ref=send_buf.at[d], dst_ref=recv_buf.at[o, e],
+            send_sem=go_send.at[d], recv_sem=go_recv.at[o, e],
+            device_id=(d, o), device_id_type=MESH,
+        )
+
+    def slot_copy(s, d, sem, target):
+        return pltpu.make_async_remote_copy(
+            src_ref=recv_buf.at[s, d], dst_ref=recv_buf.at[s, d],
+            send_sem=sem, recv_sem=go_recv.at[s, d],
+            device_id=(e, target), device_id_type=MESH,
+        )
+
+    def ps_copy(step):
+        target = lax.rem(o + step, n_orb)
+        return pltpu.make_async_remote_copy(
+            src_ref=ps_all.at[o], dst_ref=ps_all.at[o],
+            send_sem=ps_send.at[step], recv_sem=ps_recv.at[o],
+            device_id=(e, target), device_id_type=MESH,
+        )
+
+    def ps_wait(step):
+        s = lax.rem(o + step, n_orb)
+        pltpu.make_async_remote_copy(
+            src_ref=ps_all.at[s], dst_ref=ps_all.at[s],
+            send_sem=ps_send.at[step], recv_sem=ps_recv.at[s],
+            device_id=(e, s), device_id_type=MESH,
+        ).wait_recv()
+
+    started = []
+
+    def launch(copy):
+        copy.start()
+        started.append(copy)
+
+    def spread(d):
+        for j in range(1, pairs):
+            target = lax.rem(pair + j, pairs) * 2 + core
+            launch(slot_copy(o, d, cross_send.at[j, d], target))
+        launch(slot_copy(o, d, core_send.at[0, d], mate))
+
+    def pass_on(d):
+        for j in range(1, pairs):
+            s = lax.rem(pair + j, pairs) * 2 + core
+            slot_copy(s, d, core_send.at[j, d], mate).wait_recv()
+            launch(slot_copy(s, d, core_send.at[j, d], mate))
+
+    for step in order:
+        launch(go(step))
+    spread(e)
+    for step in range(1, n_orb):
+        launch(ps_copy(step))
+
+    def pick_rows(t):
+        if t == 0:
+            w_copy.wait()
+        base = t * tile
+        own = ps_all[o][0:1, :]
+        rank = lax.broadcasted_iota(jnp.int32, (tile, local), 0) + base
+        hit = rank == own
+        lane_block = lax.broadcasted_iota(jnp.int32, (tile, local), 1) // rows_block
+        row_block[base:base + tile, :] = jnp.broadcast_to(
+            jnp.sum(jnp.where(hit, lane_block, 0).astype(jnp.float32), axis=1, keepdims=True), (tile, 128)
+        )
+        row_size[base:base + tile, :] = jnp.broadcast_to(
+            jnp.sum(jnp.where(hit, size_ref[0:1, :], 0).astype(jnp.float32), axis=1, keepdims=True), (tile, 128)
+        )
+        chosen = jnp.where(hit, 1.0, 0.0).astype(jnp.bfloat16)
+        total = None
+        for c in range(blocks):
+            term = jnp.dot(
+                chosen[:, c * rows_block:(c + 1) * rows_block], w_buf[c],
+                preferred_element_type=jnp.float32,
+            )
+            total = term if total is None else total + term
+        picked[base:base + tile, :] = total.astype(jnp.bfloat16)
+
+    def mix_columns(step):
+        s = lax.rem(o + step, n_orb)
+        if step > 0:
+            ps_wait(step)
+        source = ps_all[s][0:1, :]
+
+        def heat(t, carry):
+            at = pl.ds(pl.multiple_of(t * quota, quota), quota)
+            rank = lax.broadcasted_iota(jnp.int32, (quota, local), 0) + t * quota
+            hot[at, :] = jnp.where(rank == source, 1.0, 0.0).astype(jnp.bfloat16)
+            return carry
+
+        lax.fori_loop(0, n_chan, heat, 0)
+
+        def part(t, carry):
+            at = pl.ds(pl.multiple_of(t * tile, tile), tile)
+            mine = picked[at, pl.ds(pl.multiple_of(s * rows_block, rows_block), rows_block)].astype(jnp.float32)
+            which = row_block[at, 0:1]
+            total = None
+            for c in range(blocks):
+                left = jnp.where(which == c, mine, 0.0).astype(jnp.bfloat16)
+                term = lax.dot_general(
+                    left, hot[:, c * rows_block:(c + 1) * rows_block],
+                    (((1,), (1,)), ((), ())), preferred_element_type=jnp.float32,
+                )
+                total = term if total is None else total + term
+            mix[s, at, :] = total.astype(jnp.bfloat16)
+            return carry
+
+        lax.fori_loop(0, rows // tile, part, 0)
+
+    pieces = [functools.partial(pick_rows, t) for t in range(rows // tile)]
+    pieces += [functools.partial(mix_columns, s) for s in range(n_orb)]
+    arrivals = [peer_of(e, step, n_chan) for step in order]
+    known = [e]
+    for k in range(max(len(pieces), len(arrivals))):
+        if k < len(pieces):
+            pieces[k]()
+        if k < len(arrivals):
+            d = arrivals[k]
+            slot_copy(o, d, core_send.at[0, d], mate).wait_recv()
+            spread(d)
+            pass_on(known[-1])
+            known.append(d)
+    pass_on(known[-1])
+    for d in known:
+        for j in range(pairs):
+            s = lax.rem(pair + j, pairs) * 2 + (1 - core)
+            slot_copy(s, d, core_send.at[j, d], mate).wait_recv()
+
+    half = n_chan // 2
+    columns = 256
+
+    def back(d):
+        return pltpu.make_async_remote_copy(
+            src_ref=back_buf.at[d], dst_ref=out_ref.at[e],
+            send_sem=back_send.at[d], recv_sem=back_recv.at[e],
+            device_id=(d, o), device_id_type=MESH,
+        )
+
+    for g in range(half):
+        first = lax.rem(lax.div(e, 2) + half // 2 + g, half) * 2
+        at = pl.ds(pl.multiple_of(first * quota, tile), tile)
+
+        def product(n, carry):
+            cols = pl.ds(pl.multiple_of(n * columns, columns), columns)
+            total = None
+            for s in range(n_orb):
+                term = jnp.dot(
+                    mix[s, at, :], recv_buf[s, :, :, cols].reshape(rows, columns),
+                    preferred_element_type=jnp.float32,
+                )
+                total = term if total is None else total + term
+            k = lax.broadcasted_iota(jnp.int32, (tile, columns), 1) + n * columns
+            rank = n_orb * lax.rem(k, rows_block) + lax.div(k, rows_block)
+            kept = jnp.where(rank.astype(jnp.float32) < row_size[at, 0:1], total, 0.0)
+            back_buf[pl.ds(first, 2), :, cols] = kept.astype(jnp.bfloat16).reshape(2, quota, columns)
+            return carry
+
+        lax.fori_loop(0, width // columns, product, 0)
+        for i in range(2):
+            if g == half // 2:
+                continue
+            launch(back(first + i))
+        if g == half // 2:
+            launch(back(peer_of(e, 1, n_chan)))
+            out_ref[e] = back_buf[e]
+
+    for step in range(1, n_chan):
+        d = peer_of(e, step, n_chan)
+        pltpu.make_async_remote_copy(
+            src_ref=back_buf.at[d], dst_ref=out_ref.at[d],
+            send_sem=back_send.at[d], recv_sem=back_recv.at[d],
+            device_id=(d, o), device_id_type=MESH,
+        ).wait_recv()
+    for copy in started:
+        copy.wait_send()
+
+
+def fused(amplitudes, recoupling, interaction, pair_source, channel_sizes):
+    n_chan, n_orb = lax.axis_size("chan"), lax.axis_size("orb")
+    rows, width = amplitudes.shape
+    quota = rows // n_chan
+    blocks, rows_block = pair_source.shape
+    local = blocks * rows_block
+    bf16, f32 = jnp.bfloat16, jnp.float32
+    vmem = pl.BlockSpec(memory_space=pltpu.VMEM)
+    dma = pltpu.SemaphoreType.DMA
+    source = jnp.broadcast_to(pair_source.reshape(1, local), (8, local))
+    sizes = jnp.broadcast_to(jnp.repeat(channel_sizes, rows_block)[None, :], (8, local))
+    out = pl.pallas_call(
+        functools.partial(kernel, n_chan, n_orb),
+        out_shape=jax.ShapeDtypeStruct((n_chan, quota, width), bf16),
+        in_specs=[vmem] * 4 + [pl.BlockSpec(memory_space=pl.ANY)],
+        out_specs=vmem,
+        scratch_shapes=[
+            pltpu.VMEM((n_chan, quota, width), bf16),
+            pltpu.VMEM((n_orb, n_chan, quota, width), bf16),
+            pltpu.VMEM((n_orb, 8, local), jnp.int32),
+            pltpu.VMEM(interaction.shape, bf16),
+            pltpu.VMEM((n_orb, rows, rows), bf16),
+            pltpu.VMEM((rows, local), bf16),
+            pltpu.VMEM((rows, width), bf16),
+            pltpu.VMEM((rows, 128), f32),
+            pltpu.VMEM((rows, 128), f32),
+            pltpu.VMEM((n_chan, quota, width), bf16),
+            dma,
+            dma((n_orb,)),
+            dma((n_orb,)),
+            dma((n_chan,)),
+            dma((n_orb, n_chan)),
+            dma((n_orb // 2, n_chan)),
+            dma((n_orb // 2, n_chan)),
+            dma((n_chan,)),
+            dma((n_chan,)),
+        ],
+        compiler_params=pltpu.CompilerParams(
+            collective_id=0, has_side_effects=True, vmem_limit_bytes=48 * 1024 * 1024
+        ),
+        name="cycle",
+    )(amplitudes, recoupling[:, None], source, sizes, interaction)
+    return out.reshape(rows, width)
+
+
+def exchanged(amplitudes, recoupling, interaction, pair_source, return_slot, channel_sizes):
     chan_count = lax.axis_size("chan")
     orb_count = lax.axis_size("orb")
     row_count = amplitudes.shape[0]
@@ -47,6 +336,29 @@
         tiled=True,
     )
     returned = returned.reshape(row_count, width)
+    return returned
+
+
+def fits(amplitudes, pair_source):
+    n_chan, n_orb = lax.axis_size("chan"), lax.axis_size("orb")
+    rows, width = amplitudes.shape
+    quota = rows // n_chan
+    rows_block = pair_source.shape[1]
+    return (
+        quota % 16 == 0 and rows % 128 == 0 and n_chan % 4 == 0 and n_chan & (n_chan - 1) == 0
+        and n_orb % 2 == 0 and rows_block % 128 == 0 and width % 256 == 0 and n_chan <= 16
+    )
+
+
+def shards(
+    amplitudes, recoupling, denominators, interaction, pair_source, return_slot, channel_sizes
+):
+    if fits(amplitudes, pair_source):
+        returned = fused(amplitudes, recoupling, interaction, pair_source, channel_sizes)
+    else:
+        returned = exchanged(
+            amplitudes, recoupling, interaction, pair_source, return_slot, channel_sizes
+        )
     updated = (
         amplitudes.astype(jnp.float32)
         + recoupling[:, None] * returned.astype(jnp.float32) / denominators[:, None]

time: 173 us -> 86.1 us (0.50)
  the two profiles are of different devices: /device:TPU:0 before, /device:TPU:13 now
where the time goes in v1:
time: 86.1 us; the launch traced here: 85.8 us
  Pallas kernels  79.6 us (92%)
  local copies, waits for them, and re-layouts  4.53 us (5%)
  other arithmetic  1.61 us (2%)
    pallas_call x1, Pallas kernels, fused(): pl.pallas_call(functools.partial(kernel, n_chan, n_orb), out_shape=jax.Sh...  79.6 us
    unnamed x13, local copies, waits for them, and re-layouts  3.69 us

profile of v1, /device:TPU:13, one launch (start us, length us, event | category | flops | bytes accessed | tf_op | source)
XLA Modules:
  0.0 85.8 jit_solution(1808215632969329720)
XLA Ops:
  0.0 0.0 copy-start
  0.0 0.7 copy.8
  0.7 0.0 copy-done
  0.7 0.1 broadcast_bitcast_fusion
  0.8 0.8 broadcast_in_dim.28.rec_ref
  1.6 0.0 copy-start.1
  1.6 1.3 %copy-done.1 = bf16[640,1024]{1,0:T(8,128)(2,1)S(1)} copy-done((bf16[640,1024]{1,0:T(8,128)(2,1)S(1)}, bf16[640,1024]{1,0:T(8,128)(2,1)}, u32[]{:S(2)}) %copy-start.1) | copy-done | bytes 1310744
  3.0 0.0 copy-start.2
  3.0 1.6 %copy-done.2 = bf16[4,256,1024]{2,1,0:T(8,128)(2,1)S(1)} copy-done((bf16[4,256,1024]{2,1,0:T(8,128)(2,1)S(1)}, bf16[4,256,1024]{2,1,0:T(8,128)(2,1)}, u32[]{:S(2)}) %copy-start.2) | copy-done | bytes 2097176
  4.5 0.0 copy-start.3
  4.5 0.0 copy-start.4
  4.5 79.6 %cycle.1 = bf16[8,80,1024]{2,1,0:T(8,128)(2,1)S(1)} custom-call(bf16[640,1024]{1,0:T(8,128)(2,1)S(1)} %copy-done.1, f32[640,1]{1,0:T(8,128)S(1)} %broadcast_in_dim.28.rec_ref, s32[8,1024]{1,0:T(8,128)S(1)} %broadcast_in_dim.24.ps_ref, s32[8,1024]{1,0:T(8,128)S(1)} %broadcast_in_dim.27.size_ref, bf16[4,256,1024]{2,1,0:T(8,128)(2,1)S(1)} %copy-done.2), custom_call_target="tpu_custom_call" | custom-call | tf_op jit(solution)/shard_map/cycle/pallas_call | solution.py:264
  84.2 0.0 copy-done.3
  84.2 0.0 copy-done.4
  84.2 1.6 %fusion.2 = bf16[640,1024]{1,0:T(8,128)(2,1)} fusion(bf16[640,1024]{1,0:T(8,128)(2,1)S(1)} %copy-done.1, bf16[8,80,1024]{2,1,0:T(8,128)(2,1)S(1)} %cycle.1, f32[640]{0:T(1024)S(1)} %copy-done.4, f32[640]{0:T(1024)S(1)} %copy-done.3), kind=kLoop, calls=%fused_computation.3 | loop fusion | flops 3932160 | bytes 3937280 | tf_op jit(solution)/shard_map/convert_element_type | solution.py:366
  (3 shorter events, 0.0 us)
Async XLA Ops:
  0.0 0.7 copy-start
  1.6 1.3 %copy-start.1 = (bf16[640,1024]{1,0:T(8,128)(2,1)S(1)}, bf16[640,1024]{1,0:T(8,128)(2,1)}, u32[]{:S(2)}) copy-start(bf16[640,1024]{1,0:T(8,128)(2,1)} %amp_ref.1) | copy-start | bytes 3932164
  3.0 1.6 %copy-start.2 = (bf16[4,256,1024]{2,1,0:T(8,128)(2,1)S(1)}, bf16[4,256,1024]{2,1,0:T(8,128)(2,1)}, u32[]{:S(2)}) copy-start(bf16[4,256,1024]{2,1,0:T(8,128)(2,1)} %w_ref.1) | copy-start | bytes 6291460
  4.5 79.7 %copy-start.3 = (f32[640]{0:T(1024)S(1)}, f32[640]{0:T(1024)}, u32[]{:S(2)}) copy-start(f32[640]{0:T(1024)} %param.8) | copy-start | bytes 7684
  4.5 79.7 %copy-start.4 = (f32[640]{0:T(1024)S(1)}, f32[640]{0:T(1024)}, u32[]{:S(2)}) copy-start(f32[640]{0:T(1024)} %param.9) | copy-start | bytes 7684

commit v2 on v1

--- a/solution.py
+++ b/solution.py
@@ -19,18 +19,10 @@
     return total
 
 
-def step_order(count):
-    steps = list(range(1, count))
-    far = [s for s in steps if s >= count // 2]
-    near = [s for s in steps if 1 < s < count // 2]
-    first = [s for s in steps if s == 1 and s < count // 2]
-    return first + far + near
-
-
 def kernel(
     n_chan, n_orb, amp_ref, rec_ref, ps_ref, size_ref, w_ref, out_ref,
-    send_buf, recv_buf, ps_all, w_buf, mix, hot, picked, row_block, row_size, back_buf,
-    w_sem, ps_send, ps_recv, go_send, go_recv, cross_send, core_send, back_send, back_recv,
+    amp_buf, weight, total_buf, send_buf, recv_buf, ps_all, w_buf, mix, hot, picked, row_block,
+    row_size, back_buf, amp_sem, w_sem, ps_send, ps_recv, go_send, go_recv, cross_send, core_send, back_send, back_recv,
 ):
     e = lax.axis_index("chan")
     o = lax.axis_index("orb")
@@ -43,8 +35,11 @@
     pair = lax.div(o, 2)
     mate = o + 1 - 2 * core
     tile = 2 * quota
-    order = step_order(n_chan)
-
+    half = n_chan // 2
+    order = list(range(1, n_chan))
+
+    amp_copy = pltpu.make_async_copy(amp_ref, amp_buf, amp_sem)
+    amp_copy.start()
     w_copy = pltpu.make_async_copy(w_ref, w_buf, w_sem)
     w_copy.start()
 
@@ -60,16 +55,12 @@
 
     def relay(d):
         at = pl.ds(pl.multiple_of(d * quota, quota), quota)
-        return (amp_ref[at, :].astype(jnp.float32) * rec_ref[at, :]).astype(jnp.bfloat16)
-
+        return (amp_buf[at, :].astype(jnp.float32) * weight[at, 0:1]).astype(jnp.bfloat16)
+
+    weight[...] = jnp.broadcast_to(rec_ref[0:1, :], (128, rows)).T
+    ps_all[o] = ps_ref[...]
+    amp_copy.wait()
     recv_buf[o, e] = relay(e)
-
-    def fill(d, carry):
-        send_buf[d] = relay(d)
-        return carry
-
-    lax.fori_loop(0, n_chan, fill, 0)
-    ps_all[o] = ps_ref[...]
     pl.semaphore_wait(barrier, n_chan + n_orb - 2)
 
     def go(step):
@@ -121,9 +112,11 @@
             slot_copy(s, d, core_send.at[j, d], mate).wait_recv()
             launch(slot_copy(s, d, core_send.at[j, d], mate))
 
+    spread(e)
     for step in order:
+        d = peer_of(e, step, n_chan)
+        send_buf[d] = relay(d)
         launch(go(step))
-    spread(e)
     for step in range(1, n_orb):
         launch(ps_copy(step))
 
@@ -169,40 +162,82 @@
             at = pl.ds(pl.multiple_of(t * tile, tile), tile)
             mine = picked[at, pl.ds(pl.multiple_of(s * rows_block, rows_block), rows_block)].astype(jnp.float32)
             which = row_block[at, 0:1]
-            total = None
-            for c in range(blocks):
-                left = jnp.where(which == c, mine, 0.0).astype(jnp.bfloat16)
-                term = lax.dot_general(
-                    left, hot[:, c * rows_block:(c + 1) * rows_block],
-                    (((1,), (1,)), ((), ())), preferred_element_type=jnp.float32,
-                )
+            lefts = [jnp.where(which == c, mine, 0.0).astype(jnp.bfloat16) for c in range(blocks)]
+            for h in range(half):
+                total = None
+                for c in range(blocks):
+                    term = lax.dot_general(
+                        lefts[c],
+                        hot[h * tile:(h + 1) * tile, c * rows_block:(c + 1) * rows_block],
+                        (((1,), (1,)), ((), ())), preferred_element_type=jnp.float32,
+                    )
+                    total = term if total is None else total + term
+                mix[s, h, at, :] = total.astype(jnp.bfloat16)
+            return carry
+
+        lax.fori_loop(0, rows // tile, part, 0)
+
+    columns = 256
+    here = lax.div(e, 2)
+
+    def slab(group, at, cols):
+        z = peer_of(here, group, half)
+        total = None
+        for s in range(n_orb):
+            term = jnp.dot(
+                mix[s, z, at, :],
+                recv_buf[s, pl.ds(2 * z, 2), :, cols].reshape(tile, columns),
+                preferred_element_type=jnp.float32,
+            )
+            total = term if total is None else total + term
+        return total
+
+    def gather_group(group):
+        for i in range(2):
+            d = peer_of(e, 2 * group + i, n_chan)
+            for j in range(pairs):
+                s = lax.rem(pair + j, pairs) * 2 + (1 - core)
+                slot_copy(s, d, core_send.at[j, d], mate).wait_recv()
+
+    def add_groups(groups, fresh):
+        for group in groups:
+            gather_group(group)
+
+        def block_of(t, carry):
+            at = pl.ds(pl.multiple_of(lax.div(t, width // columns) * tile, tile), tile)
+            cols = pl.ds(
+                pl.multiple_of(lax.rem(t, width // columns) * columns, columns), columns
+            )
+            total = None if fresh else total_buf[at, cols]
+            for group in groups:
+                term = slab(group, at, cols)
                 total = term if total is None else total + term
-            mix[s, at, :] = total.astype(jnp.bfloat16)
+            total_buf[at, cols] = total
             return carry
 
-        lax.fori_loop(0, rows // tile, part, 0)
-
-    pieces = [functools.partial(pick_rows, t) for t in range(rows // tile)]
-    pieces += [functools.partial(mix_columns, s) for s in range(n_orb)]
-    arrivals = [peer_of(e, step, n_chan) for step in order]
-    known = [e]
-    for k in range(max(len(pieces), len(arrivals))):
-        if k < len(pieces):
-            pieces[k]()
-        if k < len(arrivals):
-            d = arrivals[k]
-            slot_copy(o, d, core_send.at[0, d], mate).wait_recv()
-            spread(d)
-            pass_on(known[-1])
-            known.append(d)
-    pass_on(known[-1])
-    for d in known:
-        for j in range(pairs):
-            s = lax.rem(pair + j, pairs) * 2 + (1 - core)
-            slot_copy(s, d, core_send.at[j, d], mate).wait_recv()
-
-    half = n_chan // 2
-    columns = 256
+        lax.fori_loop(0, half * (width // columns), block_of, 0)
+
+    near = list(range(half // 2))
+    middle = list(range(half // 2, half - 1))
+    last = half - 1
+    stages = {k: [] for k in range(1, n_chan)}
+    stages[1] += [functools.partial(pick_rows, t) for t in range(half)]
+    for s in range(n_orb):
+        stages[min(2 + s, n_chan - 1)].append(functools.partial(mix_columns, s))
+    stages[n_chan - 1].append(functools.partial(add_groups, near, True))
+    previous = e
+    for step in order:
+        for piece in stages[step]:
+            piece()
+        d = peer_of(e, step, n_chan)
+        slot_copy(o, d, core_send.at[0, d], mate).wait_recv()
+        spread(d)
+        pass_on(previous)
+        previous = d
+    if middle:
+        add_groups(middle, False)
+    pass_on(previous)
+    gather_group(last)
 
     def back(d):
         return pltpu.make_async_remote_copy(
@@ -217,13 +252,7 @@
 
         def product(n, carry):
             cols = pl.ds(pl.multiple_of(n * columns, columns), columns)
-            total = None
-            for s in range(n_orb):
-                term = jnp.dot(
-                    mix[s, at, :], recv_buf[s, :, :, cols].reshape(rows, columns),
-                    preferred_element_type=jnp.float32,
-                )
-                total = term if total is None else total + term
+            total = total_buf[at, cols] + slab(last, at, cols)
             k = lax.broadcasted_iota(jnp.int32, (tile, columns), 1) + n * columns
             rank = n_orb * lax.rem(k, rows_block) + lax.div(k, rows_block)
             kept = jnp.where(rank.astype(jnp.float32) < row_size[at, 0:1], total, 0.0)
@@ -258,25 +287,31 @@
     local = blocks * rows_block
     bf16, f32 = jnp.bfloat16, jnp.float32
     vmem = pl.BlockSpec(memory_space=pltpu.VMEM)
+    hbm = pl.BlockSpec(memory_space=pltpu.HBM)
     dma = pltpu.SemaphoreType.DMA
+    weights = jnp.broadcast_to(recoupling[None, :], (8, rows))
     source = jnp.broadcast_to(pair_source.reshape(1, local), (8, local))
     sizes = jnp.broadcast_to(jnp.repeat(channel_sizes, rows_block)[None, :], (8, local))
     out = pl.pallas_call(
         functools.partial(kernel, n_chan, n_orb),
         out_shape=jax.ShapeDtypeStruct((n_chan, quota, width), bf16),
-        in_specs=[vmem] * 4 + [pl.BlockSpec(memory_space=pl.ANY)],
+        in_specs=[hbm] + [vmem] * 3 + [hbm],
         out_specs=vmem,
         scratch_shapes=[
+            pltpu.VMEM((rows, width), bf16),
+            pltpu.VMEM((rows, 128), f32),
+            pltpu.VMEM((rows, width), f32),
             pltpu.VMEM((n_chan, quota, width), bf16),
             pltpu.VMEM((n_orb, n_chan, quota, width), bf16),
             pltpu.VMEM((n_orb, 8, local), jnp.int32),
             pltpu.VMEM(interaction.shape, bf16),
-            pltpu.VMEM((n_orb, rows, rows), bf16),
+            pltpu.VMEM((n_orb, n_chan // 2, rows, 2 * quota), bf16),
             pltpu.VMEM((rows, local), bf16),
             pltpu.VMEM((rows, width), bf16),
             pltpu.VMEM((rows, 128), f32),
             pltpu.VMEM((rows, 128), f32),
             pltpu.VMEM((n_chan, quota, width), bf16),
+            dma,
             dma,
             dma((n_orb,)),
             dma((n_orb,)),
@@ -291,7 +326,7 @@
             collective_id=0, has_side_effects=True, vmem_limit_bytes=48 * 1024 * 1024
         ),
         name="cycle",
-    )(amplitudes, recoupling[:, None], source, sizes, interaction)
+    )(amplitudes, weights, source, sizes, interaction)
     return out.reshape(rows, width)
 
 

time: 86.1 us -> 80.6 us (0.936)
  Pallas kernels: 79.6 us -> 74.3 us
    pallas_call x1, Pallas kernels: 79.6 us -> 74.3 us  [fused(): pl.pallas_call(functools.partial(kernel, n_chan, n_orb), out_shape=jax.Sh...]
where the time goes in v2:
time: 80.6 us; the launch traced here: 80.4 us
  Pallas kernels  74.3 us (92%)
  local copies, waits for them, and re-layouts  4.39 us (5%)
  other arithmetic  1.63 us (2%)
    pallas_call x1, Pallas kernels, fused(): pl.pallas_call(functools.partial(kernel, n_chan, n_orb), out_shape=jax.Sh...  74.3 us
    unnamed x13, local copies, waits for them, and re-layouts  3.69 us
    convert_element_type x1, other arithmetic, shards(): return updated.astype(jnp.bfloat16)  1.63 us

profile of v2, /device:TPU:13, one launch (start us, length us, event | category | flops | bytes accessed | tf_op | source)
XLA Modules:
  0.0 80.4 jit_solution(17070458376907332801)
XLA Ops:
  0.0 0.0 copy-start
  0.0 0.7 copy.7
  0.7 0.0 copy-done
  0.7 0.1 broadcast_bitcast_fusion
  0.8 0.7 broadcast_in_dim.12.rec_ref
  1.5 0.0 copy-start.1
  1.5 1.3 %copy-done.1 = bf16[640,1024]{1,0:T(8,128)(2,1)S(1)} copy-done((bf16[640,1024]{1,0:T(8,128)(2,1)S(1)}, bf16[640,1024]{1,0:T(8,128)(2,1)}, u32[]{:S(2)}) %copy-start.1) | copy-done | bytes 1310744
  2.8 0.0 copy-start.2
  2.8 1.6 %copy-done.2 = bf16[4,256,1024]{2,1,0:T(8,128)(2,1)S(1)} copy-done((bf16[4,256,1024]{2,1,0:T(8,128)(2,1)S(1)}, bf16[4,256,1024]{2,1,0:T(8,128)(2,1)}, u32[]{:S(2)}) %copy-start.2) | copy-done | bytes 2097176
  4.4 0.0 copy-start.3
  4.4 0.0 copy-start.4
  4.4 74.3 %cycle.1 = bf16[8,80,1024]{2,1,0:T(8,128)(2,1)S(1)} custom-call(bf16[640,1024]{1,0:T(8,128)(2,1)S(1)} %copy-done.1, f32[8,640]{1,0:T(8,128)S(1)} %broadcast_in_dim.12.rec_ref, s32[8,1024]{1,0:T(8,128)S(1)} %broadcast_in_dim.27.ps_ref, s32[8,1024]{1,0:T(8,128)S(1)} %broadcast_in_dim.30.size_ref, bf16[4,256,1024]{2,1,0:T(8,128)(2,1)S(1)} %copy-done.2), custom_call_target="tpu_custom_call" | custom-call | tf_op jit(solution)/shard_map/cycle/pallas_call | solution.py:295
  78.7 0.0 copy-done.3
  78.7 0.0 copy-done.4
  78.7 1.6 %fusion.2 = bf16[640,1024]{1,0:T(8,128)(2,1)} fusion(bf16[640,1024]{1,0:T(8,128)(2,1)S(1)} %copy-done.1, bf16[8,80,1024]{2,1,0:T(8,128)(2,1)S(1)} %cycle.1, f32[640]{0:T(1024)S(1)} %copy-done.4, f32[640]{0:T(1024)S(1)} %copy-done.3), kind=kLoop, calls=%fused_computation.3 | loop fusion | flops 3932160 | bytes 3937280 | tf_op jit(solution)/shard_map/convert_element_type | solution.py:401
  (3 shorter events, 0.0 us)
Async XLA Ops:
  0.0 0.7 copy-start
  1.5 1.3 %copy-start.1 = (bf16[640,1024]{1,0:T(8,128)(2,1)S(1)}, bf16[640,1024]{1,0:T(8,128)(2,1)}, u32[]{:S(2)}) copy-start(bf16[640,1024]{1,0:T(8,128)(2,1)} %amp_ref.1) | copy-start | bytes 3932164
  2.8 1.6 %copy-start.2 = (bf16[4,256,1024]{2,1,0:T(8,128)(2,1)S(1)}, bf16[4,256,1024]{2,1,0:T(8,128)(2,1)}, u32[]{:S(2)}) copy-start(bf16[4,256,1024]{2,1,0:T(8,128)(2,1)} %w_ref.1) | copy-start | bytes 6291460
  4.4 74.3 %copy-start.3 = (f32[640]{0:T(1024)S(1)}, f32[640]{0:T(1024)}, u32[]{:S(2)}) copy-start(f32[640]{0:T(1024)} %param.8) | copy-start | bytes 7684
  4.4 74.3 %copy-start.4 = (f32[640]{0:T(1024)S(1)}, f32[640]{0:T(1024)}, u32[]{:S(2)}) copy-start(f32[640]{0:T(1024)} %param.9) | copy-start | bytes 7684

commit v3 on v2

--- a/solution.py
+++ b/solution.py
@@ -178,6 +178,7 @@
         lax.fori_loop(0, rows // tile, part, 0)
 
     columns = 256
+    span = rows // 1
     here = lax.div(e, 2)
 
     def slab(group, at, cols):
@@ -204,7 +205,7 @@
             gather_group(group)
 
         def block_of(t, carry):
-            at = pl.ds(pl.multiple_of(lax.div(t, width // columns) * tile, tile), tile)
+            at = pl.ds(pl.multiple_of(lax.div(t, width // columns) * span, span), span)
             cols = pl.ds(
                 pl.multiple_of(lax.rem(t, width // columns) * columns, columns), columns
             )
@@ -215,7 +216,7 @@
             total_buf[at, cols] = total
             return carry
 
-        lax.fori_loop(0, half * (width // columns), block_of, 0)
+        lax.fori_loop(0, rows // span * (width // columns), block_of, 0)
 
     near = list(range(half // 2))
     middle = list(range(half // 2, half - 1))

time: 80.6 us -> 78.5 us (0.974)
  Pallas kernels: 74.3 us -> 72.2 us
    pallas_call x1, Pallas kernels: 74.3 us -> 72.2 us  [fused(): pl.pallas_call(functools.partial(kernel, n_chan, n_orb), out_shape=jax.Sh...]
where the time goes in v3:
time: 78.5 us; the launch traced here: 78.2 us
  Pallas kernels  72.2 us (92%)
  local copies, waits for them, and re-layouts  4.39 us (6%)
  other arithmetic  1.63 us (2%)
    pallas_call x1, Pallas kernels, fused(): pl.pallas_call(functools.partial(kernel, n_chan, n_orb), out_shape=jax.Sh...  72.2 us
    unnamed x13, local copies, waits for them, and re-layouts  3.69 us
    convert_element_type x1, other arithmetic, shards(): return updated.astype(jnp.bfloat16)  1.63 us

profile of v3, /device:TPU:13, one launch (start us, length us, event | category | flops | bytes accessed | tf_op | source)
XLA Modules:
  0.0 78.2 jit_solution(8787028606468619669)
XLA Ops:
  0.0 0.0 copy-start
  0.0 0.7 copy.7
  0.7 0.0 copy-done
  0.7 0.1 broadcast_bitcast_fusion
  0.8 0.7 broadcast_in_dim.12.rec_ref
  1.5 0.0 copy-start.1
  1.5 1.3 %copy-done.1 = bf16[640,1024]{1,0:T(8,128)(2,1)S(1)} copy-done((bf16[640,1024]{1,0:T(8,128)(2,1)S(1)}, bf16[640,1024]{1,0:T(8,128)(2,1)}, u32[]{:S(2)}) %copy-start.1) | copy-done | bytes 1310744
  2.8 0.0 copy-start.2
  2.8 1.6 %copy-done.2 = bf16[4,256,1024]{2,1,0:T(8,128)(2,1)S(1)} copy-done((bf16[4,256,1024]{2,1,0:T(8,128)(2,1)S(1)}, bf16[4,256,1024]{2,1,0:T(8,128)(2,1)}, u32[]{:S(2)}) %copy-start.2) | copy-done | bytes 2097176
  4.4 0.0 copy-start.3
  4.4 0.0 copy-start.4
  4.4 72.2 %cycle.1 = bf16[8,80,1024]{2,1,0:T(8,128)(2,1)S(1)} custom-call(bf16[640,1024]{1,0:T(8,128)(2,1)S(1)} %copy-done.1, f32[8,640]{1,0:T(8,128)S(1)} %broadcast_in_dim.12.rec_ref, s32[8,1024]{1,0:T(8,128)S(1)} %broadcast_in_dim.27.ps_ref, s32[8,1024]{1,0:T(8,128)S(1)} %broadcast_in_dim.30.size_ref, bf16[4,256,1024]{2,1,0:T(8,128)(2,1)S(1)} %copy-done.2), custom_call_target="tpu_custom_call" | custom-call | tf_op jit(solution)/shard_map/cycle/pallas_call | solution.py:296
  76.6 0.0 copy-done.3
  76.6 0.0 copy-done.4
  76.6 1.6 %fusion.2 = bf16[640,1024]{1,0:T(8,128)(2,1)} fusion(bf16[640,1024]{1,0:T(8,128)(2,1)S(1)} %copy-done.1, bf16[8,80,1024]{2,1,0:T(8,128)(2,1)S(1)} %cycle.1, f32[640]{0:T(1024)S(1)} %copy-done.4, f32[640]{0:T(1024)S(1)} %copy-done.3), kind=kLoop, calls=%fused_computation.3 | loop fusion | flops 3932160 | bytes 3937280 | tf_op jit(solution)/shard_map/convert_element_type | solution.py:402
  (3 shorter events, 0.0 us)
Async XLA Ops:
  0.0 0.7 copy-start
  1.5 1.3 %copy-start.1 = (bf16[640,1024]{1,0:T(8,128)(2,1)S(1)}, bf16[640,1024]{1,0:T(8,128)(2,1)}, u32[]{:S(2)}) copy-start(bf16[640,1024]{1,0:T(8,128)(2,1)} %amp_ref.1) | copy-start | bytes 3932164
  2.8 1.6 %copy-start.2 = (bf16[4,256,1024]{2,1,0:T(8,128)(2,1)S(1)}, bf16[4,256,1024]{2,1,0:T(8,128)(2,1)}, u32[]{:S(2)}) copy-start(bf16[4,256,1024]{2,1,0:T(8,128)(2,1)} %w_ref.1) | copy-start | bytes 6291460
  4.4 72.2 %copy-start.3 = (f32[640]{0:T(1024)S(1)}, f32[640]{0:T(1024)}, u32[]{:S(2)}) copy-start(f32[640]{0:T(1024)} %param.8) | copy-start | bytes 7684
  4.4 72.2 %copy-start.4 = (f32[640]{0:T(1024)S(1)}, f32[640]{0:T(1024)}, u32[]{:S(2)}) copy-start(f32[640]{0:T(1024)} %param.9) | copy-start | bytes 7684
